TPU v7x, 32 devices: a whole 2x2x4 slice. The times are simulated.
32 devices in a mesh: dp: 4 (over y, x), expert: 8 (over z, core).
Axes of the slice: x: 2, y: 2, z: 4, core: 2. Of those that a mesh axis runs over, the one named last changes fastest.
Arguments:
- tokens: bfloat16 [4096, 2048], P(('dp', 'expert')), may hold values from -6 to 6
- cotangent: bfloat16 [4096, 2048], P(('dp', 'expert')), may hold values from -6 to 6
- expert_ids: int32 [4096, 4], P(('dp', 'expert')), may hold values from 0 to 7, all different within a row; in each aligned block of 128 rows (0 to 127, 128 to 255, ...) at most 80 rows name the same one
- gate_probs: bfloat16 [4096, 4], P(('dp', 'expert')), may hold values from 0.049804688 to 1
- w_gate: bfloat16 [8, 2048, 512], P('expert', 'dp'), may hold values from -0.125 to 0.125
- w_up: bfloat16 [8, 2048, 512], P('expert', 'dp'), may hold values from -0.125 to 0.125
- w_down: bfloat16 [8, 512, 2048], P('expert', None, 'dp'), may hold values from -0.25 to 0.25
Outputs:
- mixed: bfloat16 [4096, 2048], P(('dp', 'expert'))
- grad_tokens: bfloat16 [4096, 2048], P(('dp', 'expert'))
- grad_gates: float32 [4096, 4], P(('dp', 'expert'))
- grad_gate_w: float32 [8, 2048, 512], P('expert', 'dp')
- grad_up_w: float32 [8, 2048, 512], P('expert', 'dp')
- grad_down_w: float32 [8, 512, 2048], P('expert', None, 'dp')
Inputs may be any that keep to these rules, and one draw needn't show every extreme that they name: `expert_ids`: each row names 4 different experts. Within the rows of one device (aligned blocks of 128 rows) no expert is named by more than 80 rows, a bound that some block reaches.
All inputs are finite; a program needn't handle non-finite values.
Results may differ from a plain program's by a relative error of at most 0.0085.
Values may be sent and summed in bfloat16 or wider, within the bound.
A program may use at most 128 MiB of HBM per device.

v0:
```python
import jax
import jax.numpy as jnp
from jax import lax
from jax.sharding import PartitionSpec as P


def silu_parts(pre_gate):
    sigma = jax.nn.sigmoid(pre_gate)
    return (pre_gate * sigma, sigma * (1.0 + pre_gate * (1.0 - sigma)))


def on_device(tokens, cotangent, expert_ids, gate_probs, w_gate, w_up, w_down):
    axis_count = lax.axis_size("expert")
    local_experts = w_gate.shape[0]
    tok_rows = tokens.shape[0]
    model_width = tokens.shape[1]
    top_count = expert_ids.shape[1]
    all_experts = local_experts * axis_count
    capacity = max(2, 5 * tok_rows * top_count // (4 * all_experts))
    pair_count = tok_rows * top_count
    flat_ids = expert_ids.reshape(-1)
    onehot = (flat_ids[:, None] == jnp.arange(all_experts, dtype=jnp.int32)[None, :]).astype(
        jnp.int32
    )
    earlier = jnp.cumsum(onehot, axis=0) - onehot
    slot_rank = jnp.sum(earlier * onehot, axis=1)
    position = flat_ids * capacity + slot_rank
    pair_table = jnp.full((all_experts * capacity,), pair_count, jnp.int32)
    pair_table = pair_table.at[position].set(jnp.arange(pair_count, dtype=jnp.int32))
    routed = (
        gate_probs.astype(jnp.float32)[:, :, None] * cotangent.astype(jnp.float32)[:, None, :]
    ).astype(jnp.bfloat16)
    routed = routed.reshape(pair_count, model_width)
    send_shape = (axis_count, local_experts, capacity, model_width)
    token_send = jnp.take(
        tokens, pair_table // top_count, axis=0, mode="fill", fill_value=0
    ).reshape(send_shape)
    routed_send = jnp.take(routed, pair_table, axis=0, mode="fill", fill_value=0).reshape(
        send_shape
    )
    token_recv, routed_recv = (
        lax.all_to_all(token_send, "expert", split_axis=0, concat_axis=2, tiled=True),
        lax.all_to_all(routed_send, "expert", split_axis=0, concat_axis=2, tiled=True),
    )
    rows_in = token_recv[0]
    routed_in = routed_recv[0]
    full_gate, full_up, full_down = (
        lax.all_gather(w_gate, "dp", axis=1, tiled=True),
        lax.all_gather(w_up, "dp", axis=1, tiled=True),
        lax.all_gather(w_down, "dp", axis=2, tiled=True),
    )
    pre_gate = jnp.einsum("end,edf->enf", rows_in, full_gate, preferred_element_type=jnp.float32)
    pre_up = jnp.einsum("end,edf->enf", rows_in, full_up, preferred_element_type=jnp.float32)
    activated, slope = silu_parts(pre_gate)
    hidden = (activated * pre_up).astype(jnp.bfloat16)
    expert_out = jnp.einsum(
        "enf,efd->end", hidden, full_down, preferred_element_type=jnp.float32
    ).astype(jnp.bfloat16)
    grad_hidden = jnp.einsum(
        "end,efd->enf", routed_in, full_down, preferred_element_type=jnp.float32
    )
    grad_pre_gate = (grad_hidden * pre_up * slope).astype(jnp.bfloat16)
    grad_pre_up = (grad_hidden * activated).astype(jnp.bfloat16)
    pair_grad = jnp.einsum(
        "enf,edf->end", grad_pre_gate, full_gate, preferred_element_type=jnp.float32
    )
    pair_grad = pair_grad + jnp.einsum(
        "enf,edf->end", grad_pre_up, full_up, preferred_element_type=jnp.float32
    )
    pair_grad = pair_grad.astype(jnp.bfloat16)
    back_out, back_grad = (
        lax.all_to_all(expert_out[None], "expert", split_axis=2, concat_axis=0, tiled=True),
        lax.all_to_all(pair_grad[None], "expert", split_axis=2, concat_axis=0, tiled=True),
    )
    out_pairs = back_out.reshape(all_experts * capacity, model_width)[position].reshape(
        tok_rows, top_count, model_width
    )
    grad_pairs = back_grad.reshape(all_experts * capacity, model_width)[position].reshape(
        tok_rows, top_count, model_width
    )
    mixed = jnp.einsum(
        "tk,tkd->td", gate_probs, out_pairs, preferred_element_type=jnp.float32
    ).astype(jnp.bfloat16)
    grad_gates = jnp.einsum("td,tkd->tk", cotangent, out_pairs, preferred_element_type=jnp.float32)
    grad_tokens = jnp.sum(grad_pairs.astype(jnp.float32), axis=1).astype(jnp.bfloat16)
    part_gate = jnp.einsum(
        "end,enf->edf", rows_in, grad_pre_gate, preferred_element_type=jnp.float32
    )
    part_up = jnp.einsum("end,enf->edf", rows_in, grad_pre_up, preferred_element_type=jnp.float32)
    part_down = jnp.einsum("enf,end->efd", hidden, routed_in, preferred_element_type=jnp.float32)
    grad_gate_w, grad_up_w, grad_down_w = (
        lax.psum_scatter(
            part_gate.astype(jnp.bfloat16), "dp", scatter_dimension=1, tiled=True
        ).astype(jnp.float32),
        lax.psum_scatter(
            part_up.astype(jnp.bfloat16), "dp", scatter_dimension=1, tiled=True
        ).astype(jnp.float32),
        lax.psum_scatter(
            part_down.astype(jnp.bfloat16), "dp", scatter_dimension=2, tiled=True
        ).astype(jnp.float32),
    )
    return (mixed, grad_tokens, grad_gates, grad_gate_w, grad_up_w, grad_down_w)


def solution(mesh):
    in_specs = (
        P(("dp", "expert"), None),
        P(("dp", "expert"), None),
        P(("dp", "expert"), None),
        P(("dp", "expert"), None),
        P("expert", "dp", None),
        P("expert", "dp", None),
        P("expert", None, "dp"),
    )
    out_specs = (
        P(("dp", "expert"), None),
        P(("dp", "expert"), None),
        P(("dp", "expert"), None),
        P("expert", "dp", None),
        P("expert", "dp", None),
        P("expert", None, "dp"),
    )
    return jax.shard_map(
        on_device, mesh=mesh, in_specs=in_specs, out_specs=out_specs, check_vma=False
    )
```

profile of v0, /device:TPU:0, one launch (start us, length us, event | category | flops | bytes accessed | tf_op | source)
XLA Modules:
  0.0 368.4 jit_solution(10212295184746783173)
XLA Ops:
  7.2 0.7 all-gather.4.cloned.1.call-update
  7.9 0.8 copy.26
  8.8 0.1 eq.25
  8.9 0.7 broadcast_multiply_fusion
  9.6 1.1 reduce-window.6
  10.7 0.2 slice_reduce_fusion
  11.0 0.1 copy.25
  11.1 0.1 mul.69
  11.3 2.4 scatter_custom_fusion
  13.9 3.4 gather_fusion
  17.4 1.8 broadcast_select_fusion.1
  19.1 6.5 %all-to-all-start = ((bf16[8,1,80,2048]{3,2,1,0:T(8,128)(2,1)}), bf16[8,1,80,2048]{3,2,1,0:T(8,128)(2,1)}, u32[]{:S(2)}, u32[]{:S(2)}) async-start(bf16[8,1,80,2048]{3,2,1,0:T(8,128)(2,1)} %broadcast_select_fusion.1), calls=%async_computation | async-start | bytes 5242880 | tf_op jit(solution)/shard_map/all_to_all | solution.py:42
  25.6 0.7 all-gather.6.cloned.1.call-update
  26.4 3.1 mul.76
  29.5 5.3 %mul.77 = f32[512,2048]{1,0:T(8,128)} reshape(f32[128,4,2048]{2,1,0:T(4,128)} %mul.76) | data formatting | bytes 8388608 | tf_op jit(solution)/shard_map/mul | solution.py:31
  34.8 0.1 copy.30
  34.9 0.1 reshape.222
  35.1 2.5 multiply_convert_fusion
  37.5 4.1 %gather_fusion.2 = bf16[640,2048]{1,0:T(8,128)(2,1)} fusion(bf16[512,2048]{1,0:T(8,128)(2,1)S(1)} %multiply_convert_fusion, s32[1024]{0:T(1024)S(1)} %pad_clamp_fusion), kind=kCustom, calls=%fused_computation.2 | custom fusion | bytes 5245440 | tf_op jit(solution)/shard_map/jit(_take)/gather | solution.py:38
  41.7 3.5 broadcast_select_fusion
  45.2 40.8 %all-to-all-done = bf16[8,1,80,2048]{3,2,1,0:T(8,128)(2,1)} async-done(((bf16[8,1,80,2048]{3,2,1,0:T(8,128)(2,1)}), bf16[8,1,80,2048]{3,2,1,0:T(8,128)(2,1)}, u32[]{:S(2)}, u32[]{:S(2)}) %all-to-all-start) | async-done | bytes 2621472 | tf_op jit(solution)/shard_map/all_to_all | solution.py:42
  86.0 3.6 all-to-all-start.2
  89.7 0.7 all-gather.8.cloned.1.call-update
  90.4 0.2 reduce-scatter.4.cloned.1.call-start
  90.6 5.0 %fusion.13 = f32[640,512]{1,0:T(8,128)} fusion(bf16[640,2048]{1,0:T(8,128)(2,1)} %bitcast.6, bf16[1,2048,512]{2,1,0:T(8,128)(2,1)} %all-gather.4.cloned.1.call-done), kind=kOutput, calls=%fused_computation.28 | convolution fusion | flops 1342177280 | bytes 6029312 | tf_op jit(solution)/shard_map/end,edf->enf/dot_general | solution.py:52
  95.6 4.9 %fusion.9 = f32[640,512]{1,0:T(8,128)} fusion(bf16[640,2048]{1,0:T(8,128)(2,1)} %bitcast.6, bf16[1,2048,512]{2,1,0:T(8,128)(2,1)} %all-gather.6.cloned.1.call-done), kind=kOutput, calls=%fused_computation.24 | convolution fusion | flops 1342177280 | bytes 6029312 | tf_op jit(solution)/shard_map/end,edf->enf/dot_general | solution.py:53
  100.5 28.4 %all-gather.8.cloned.1.call-done = bf16[1,512,2048]{2,1,0:T(8,128)(2,1)} async-done(((bf16[1,512,512]{2,1,0:T(8,128)(2,1)}), bf16[1,512,2048]{2,1,0:T(8,128)(2,1)}) %all-gather.8.cloned.1.call-update) | async-done | bytes 2097168 | tf_op jit(solution)/shard_map/all_gather | solution.py:50
  128.9 21.0 %all-to-all-done.2 = bf16[8,1,80,2048]{3,2,1,0:T(8,128)(2,1)S(1)} async-done(((bf16[8,1,80,2048]{3,2,1,0:T(8,128)(2,1)}), bf16[8,1,80,2048]{3,2,1,0:T(8,128)(2,1)S(1)}, u32[]{:S(2)}, u32[]{:S(2)}) %all-to-all-start.2) | async-done | bytes 2621472 | tf_op jit(solution)/shard_map/all_to_all | solution.py:43
  149.8 5.4 %multiply_convert_fusion.1 = (bf16[640,512]{1,0:T(8,128)(2,1)}, bf16[640,512]{1,0:T(8,128)(2,1)S(1)}, bf16[640,512]{1,0:T(8,128)(2,1)}) fusion(f32[640,512]{1,0:T(8,128)} %fusion.13, f32[640,512]{1,0:T(8,128)} %fusion.9, bf16[640,2048]{1,0:T(8,128)(2,1)S(1)} %bitcast.86, bf16[1,512,2048]{2,1,0:T(8,128)(2,1)} %all-gather.8.cloned.1.call-done), kind=kOutput, calls=%fused_computation.30 | convolution fusion | flops 1347092480 | bytes 9306112 | tf_op jit(solution)/shard_map/end,efd->enf/dot_general | solution.py:59
  155.2 0.8 copy-done.5
  156.1 4.9 %fusion.2 = bf16[1,2048,512]{2,1,0:T(8,128)(2,1)} fusion(bf16[640,2048]{1,0:T(8,128)(2,1)} %bitcast.6, bf16[640,512]{1,0:T(8,128)(2,1)S(1)} %get-tuple-element.9), kind=kOutput, calls=%fused_computation.13 | convolution fusion | flops 1343225856 | bytes 5373952 | tf_op jit(solution)/shard_map/end,enf->edf/dot_general | solution.py:86
  161.0 3.5 fusion.11
  164.5 3.1 fusion.1
  167.6 8.2 %copy.49 = bf16[1,1,640,2048]{3,1,0,2:T(2,128)(2,1)} copy(bf16[1,1,640,2048]{3,2,1,0:T(8,128)(2,1)} %fusion.1) | data formatting | bytes 5242880 | tf_op jit(solution)/shard_map/broadcast_in_dim | solution.py:73
  175.8 0.5 broadcast.134
  176.3 17.7 %reduce.4 = bf16[640,2048]{1,0:T(8,128)(2,1)} reduce(bf16[640,1,1,2048]{3,2,1,0:T(2,128)(2,1)} %bitcast.82, bf16[]{:T(256)} %broadcast.134), dimensions={1,2}, to_apply=%bitcast.78.reduce_sub_computation | reduce | bytes 5242882
  194.0 6.7 %reshape.274 = bf16[8,2,81920]{2,1,0:T(2,128)(2,1)} reshape(bf16[640,2048]{1,0:T(8,128)(2,1)} %reduce.4) | data formatting | bytes 5242880
  200.7 4.4 %all-to-all-start.3 = ((bf16[8,2,81920]{2,1,0:T(2,128)(2,1)}), bf16[8,2,81920]{2,1,0:T(2,128)(2,1)}, u32[]{:S(2)}, u32[]{:S(2)}) async-start(bf16[8,2,81920]{2,1,0:T(2,128)(2,1)} %reshape.274), calls=%async_computation.3 | async-start | bytes 5242880 | tf_op jit(solution)/shard_map/all_to_all | solution.py:73
  205.1 5.0 %fusion.3 = bf16[1,2048,512]{2,1,0:T(8,128)(2,1)} fusion(bf16[640,2048]{1,0:T(8,128)(2,1)} %bitcast.6, bf16[640,512]{1,0:T(8,128)(2,1)} %get-tuple-element.8), kind=kOutput, calls=%fused_computation.14 | convolution fusion | flops 1343225856 | bytes 5373952 | tf_op jit(solution)/shard_map/end,enf->edf/dot_general | solution.py:89
  210.2 4.9 %fusion = bf16[1,1,640,2048]{3,2,1,0:T(8,128)(2,1)} fusion(bf16[640,512]{1,0:T(8,128)(2,1)} %get-tuple-element.10, bf16[1,512,2048]{2,1,0:T(8,128)(2,1)} %all-gather.8.cloned.1.call-done), kind=kOutput, calls=%fused_computation.11 | convolution fusion | flops 1343488000 | bytes 5373952 | tf_op jit(solution)/shard_map/enf,efd->end/dot_general | solution.py:56
  215.1 8.0 %copy.50 = bf16[1,1,640,2048]{3,1,0,2:T(2,128)(2,1)} copy(bf16[1,1,640,2048]{3,2,1,0:T(8,128)(2,1)} %fusion) | data formatting | bytes 5242880 | tf_op jit(solution)/shard_map/broadcast_in_dim | solution.py:72
  223.1 17.6 %reduce.3 = bf16[640,2048]{1,0:T(8,128)(2,1)} reduce(bf16[640,1,1,2048]{3,2,1,0:T(2,128)(2,1)} %bitcast.83, bf16[]{:T(256)} %broadcast.134), dimensions={1,2}, to_apply=%bitcast.79.reduce_sub_computation | reduce | bytes 5242882
  240.7 6.7 %reshape.272 = bf16[8,2,81920]{2,1,0:T(2,128)(2,1)} reshape(bf16[640,2048]{1,0:T(8,128)(2,1)} %reduce.3) | data formatting | bytes 5242880
  247.4 18.0 %all-to-all-done.3 = bf16[8,2,81920]{2,1,0:T(2,128)(2,1)} async-done(((bf16[8,2,81920]{2,1,0:T(2,128)(2,1)}), bf16[8,2,81920]{2,1,0:T(2,128)(2,1)}, u32[]{:S(2)}, u32[]{:S(2)}) %all-to-all-start.3) | async-done | bytes 2621472 | tf_op jit(solution)/shard_map/all_to_all | solution.py:73
  265.4 4.8 %all-to-all-start.1 = ((bf16[8,2,81920]{2,1,0:T(2,128)(2,1)}), bf16[8,2,81920]{2,1,0:T(2,128)(2,1)}, u32[]{:S(2)}, u32[]{:S(2)}) async-start(bf16[8,2,81920]{2,1,0:T(2,128)(2,1)} %reshape.272), calls=%async_computation.1 | async-start | bytes 5242880 | tf_op jit(solution)/shard_map/all_to_all | solution.py:72
  270.3 4.2 %fusion.4 = bf16[1,512,2048]{2,1,0:T(8,128)(2,1)} fusion(bf16[640,512]{1,0:T(8,128)(2,1)} %get-tuple-element.10, bf16[640,2048]{1,0:T(8,128)(2,1)S(1)} %bitcast.87), kind=kOutput, calls=%fused_computation.15 | convolution fusion | flops 1343225856 | bytes 5373952 | tf_op jit(solution)/shard_map/enf,end->efd/dot_general | solution.py:90
  274.5 0.1 copy.33
  274.7 2.1 convert_element_type.79
  276.8 2.1 convert_element_type.82
  279.0 32.2 %reduce-scatter.8.cloned.1.call-done = bf16[1,512,512]{2,1,0:T(8,128)(2,1)} async-done(((bf16[1,512,2048]{2,1,0:T(8,128)(2,1)}), bf16[1,512,512]{2,1,0:T(8,128)(2,1)}) %reduce-scatter.8.cloned.1.call-update) | async-done | bytes 524304 | tf_op jit(solution)/shard_map/reduce_scatter | solution.py:98
  311.2 2.1 convert_element_type.85
  313.4 7.3 %reshape.275 = bf16[640,1,1,2048]{3,2,1,0:T(2,128)(2,1)} reshape(bf16[8,2,81920]{2,1,0:T(2,128)(2,1)} %all-to-all-done.3) | data formatting | bytes 5242880
  320.6 4.1 %copy.46 = bf16[1,1,640,2048]{3,2,0,1:T(8,128)(2,1)S(1)} copy(bf16[1,1,640,2048]{3,1,0,2:T(2,128)(2,1)} %bitcast.84) | data formatting | bytes 5242880
  324.7 3.3 gather_fusion.3
  328.0 4.1 %reshape.221 = bf16[128,4,2048]{2,1,0:T(4,128)(2,1)} reshape(bf16[512,2048]{1,0:T(8,128)(2,1)} %gather_fusion.3) | data formatting | bytes 4194304 | tf_op jit(solution)/shard_map/reshape | solution.py:78
  332.2 7.3 %reshape.273 = bf16[640,1,1,2048]{3,2,1,0:T(2,128)(2,1)} reshape(bf16[8,2,81920]{2,1,0:T(2,128)(2,1)} %all-to-all-done.1) | data formatting | bytes 5242880
  339.5 4.1 %copy.47 = bf16[1,1,640,2048]{3,2,0,1:T(8,128)(2,1)S(1)} copy(bf16[1,1,640,2048]{3,1,0,2:T(2,128)(2,1)} %bitcast.85) | data formatting | bytes 5242880
  343.5 3.4 gather_fusion.1
  346.9 2.9 reshape.218
  349.8 1.2 fusion.25
  351.2 1.1 copy.48
  352.3 4.6 %fusion.16 = f32[128,1,4]{2,1,0:T(1,128)S(1)} fusion(bf16[128,4,2048]{2,1,0:T(4,128)(2,1)} %copy-done.3, bf16[128,2048,1]{1,0,2:T(8,128)(2,1)S(1)} %bitcast.90), kind=kOutput, calls=%fused_computation.36 | convolution fusion | flops 2097152 | bytes 2623488 | tf_op jit(solution)/shard_map/td,tkd->tk/dot_general | solution.py:84
  356.9 0.7 copy.36
  357.5 3.9 %reduce_sum.25 = bf16[128,2048]{1,0:T(8,128)(2,1)} reduce(bf16[128,4,2048]{2,1,0:T(4,128)(2,1)S(1)} %copy-done.2, bf16[]{:T(256)} %constant.57.clone.1), dimensions={1}, to_apply=%region_4.5 | reduce | flops 786432 | bytes 2621442 | tf_op jit(solution)/shard_map/reduce_sum | solution.py:85
  (46 shorter events, 0.9 us)
Async XLA Ops:
  7.2 6.8 %copy-start = (bf16[128,2048]{1,0:T(8,128)(2,1)S(1)}, bf16[128,2048]{1,0:T(8,128)(2,1)}, u32[]{:S(2)}) copy-start(bf16[128,2048]{1,0:T(8,128)(2,1)} %param.7) | copy-start | bytes 1572868
  7.2 83.4 %all-gather.4.cloned.1.call-start = ((), (), s32[]{:S(2)}) async-start(), calls=%async_computation.7 | async-start | bytes 2621440 | tf_op jit(solution)/shard_map/all_gather | solution.py:48
  19.1 7.3 %copy-start.7 = (bf16[128,2048]{1,0:T(8,128)(2,1)S(1)}, bf16[128,2048]{1,0:T(8,128)(2,1)}, u32[]{:S(2)}) copy-start(bf16[128,2048]{1,0:T(8,128)(2,1)} %param.8) | copy-start | bytes 1572868
  19.1 66.9 %all-to-all-start = ((bf16[8,1,80,2048]{3,2,1,0:T(8,128)(2,1)}), bf16[8,1,80,2048]{3,2,1,0:T(8,128)(2,1)}, u32[]{:S(2)}, u32[]{:S(2)}) async-start(bf16[8,1,80,2048]{3,2,1,0:T(8,128)(2,1)} %broadcast_select_fusion.1), calls=%async_computation | async-start | bytes 5242880 | tf_op jit(solution)/shard_map/all_to_all | solution.py:42
  25.6 70.0 %all-gather.6.cloned.1.call-start = ((), (), s32[]{:S(2)}) async-start(), calls=%async_computation.8 | async-start | bytes 2621440 | tf_op jit(solution)/shard_map/all_gather | solution.py:49
  29.5 5.3 %copy-start.9 = (bf16[128,4]{0,1:T(4,128)(2,1)S(1)}, bf16[128,4]{0,1:T(4,128)(2,1)}, u32[]{:S(2)}) copy-start(bf16[128,4]{0,1:T(4,128)(2,1)} %param.10) | copy-start | bytes 3076
  86.0 63.9 %all-to-all-start.2 = ((bf16[8,1,80,2048]{3,2,1,0:T(8,128)(2,1)}), bf16[8,1,80,2048]{3,2,1,0:T(8,128)(2,1)S(1)}, u32[]{:S(2)}, u32[]{:S(2)}) async-start(bf16[8,1,80,2048]{3,2,1,0:T(8,128)(2,1)} %broadcast_select_fusion), calls=%async_computation.2 | async-start | bytes 5242880 | tf_op jit(solution)/shard_map/all_to_all | solution.py:43
  89.6 39.3 %all-gather.8.cloned.1.call-start = ((), (), s32[]{:S(2)}) async-start(), calls=%async_computation.9 | async-start | bytes 2621440 | tf_op jit(solution)/shard_map/all_gather | solution.py:50
  90.4 184.3 %reduce-scatter.4.cloned.1.call-start = ((), (), s32[]{:S(2)}) async-start(), calls=%async_computation.10 | async-start | bytes 2621440 | tf_op jit(solution)/shard_map/reduce_scatter | solution.py:92
  155.2 0.8 copy-start.5
  161.0 3.5 copy-start.4
  161.0 3.5 copy-start.6
  200.7 64.7 %all-to-all-start.3 = ((bf16[8,2,81920]{2,1,0:T(2,128)(2,1)}), bf16[8,2,81920]{2,1,0:T(2,128)(2,1)}, u32[]{:S(2)}, u32[]{:S(2)}) async-start(bf16[8,2,81920]{2,1,0:T(2,128)(2,1)} %reshape.274), calls=%async_computation.3 | async-start | bytes 5242880 | tf_op jit(solution)/shard_map/all_to_all | solution.py:73
  205.1 71.7 %reduce-scatter.6.cloned.1.call-start = ((), (), s32[]{:S(2)}) async-start(), calls=%async_computation.11 | async-start | bytes 2621440 | tf_op jit(solution)/shard_map/reduce_scatter | solution.py:95
  265.4 66.8 %all-to-all-start.1 = ((bf16[8,2,81920]{2,1,0:T(2,128)(2,1)}), bf16[8,2,81920]{2,1,0:T(2,128)(2,1)}, u32[]{:S(2)}, u32[]{:S(2)}) async-start(bf16[8,2,81920]{2,1,0:T(2,128)(2,1)} %reshape.272), calls=%async_computation.1 | async-start | bytes 5242880 | tf_op jit(solution)/shard_map/all_to_all | solution.py:72
  270.2 41.0 %reduce-scatter.8.cloned.1.call-start = ((), (), s32[]{:S(2)}) async-start(), calls=%async_computation.12 | async-start | bytes 2621440 | tf_op jit(solution)/shard_map/reduce_scatter | solution.py:98
  349.8 1.4 copy-start.3
  349.8 2.4 copy-start.8
  352.3 5.3 %copy-start.2 = (bf16[128,4,2048]{2,1,0:T(4,128)(2,1)S(1)}, bf16[128,4,2048]{2,1,0:T(4,128)(2,1)}, u32[]{:S(2)}) copy-start(bf16[128,4,2048]{2,1,0:T(4,128)(2,1)} %reshape.221) | copy-start | bytes 6291460
  352.3 9.1 %copy-start.1 = (bf16[128,2048]{1,0:T(8,128)(2,1)S(1)}, bf16[128,2048]{1,0:T(8,128)(2,1)}, u32[]{:S(2)}) copy-start(bf16[128,2048]{1,0:T(8,128)(2,1)} %param.7) | copy-start | bytes 1572868
Sparse Core Ops, SparseCore 0:
  9.9 38.0 all-gather.3
  49.8 35.2 all-gather.5
  92.3 36.5 all-gather.7
  161.1 34.0 reduce-scatter.3
  210.3 36.5 reduce-scatter.5
  274.6 36.5 reduce-scatter.7
where the time goes:
time: 375 us; the launch traced here: 368 us
  waiting for transfers between devices  142 us (38%)
  local copies, waits for them, and re-layouts  89.6 us (24%)
  other arithmetic  55.4 us (15%)
  matrix products  46.7 us (12%)
  starting transfers between devices  19.7 us (5%)
  between operations  14.5 us (4%)
    all_to_all x1, waiting for transfers between devices, on_device(): lax.all_to_all(token_send, 'expert', split_axis=0, concat_axis=2, tiled=T...  40.8 us
    unnamed x29, local copies, waits for them, and re-layouts  38.6 us
    unnamed x2, other arithmetic  35.3 us
    reduce_scatter x1, waiting for transfers between devices, on_device(): lax.psum_scatter(part_down.astype(jnp.bfloat16), 'dp', scatter_dimension=...  32.2 us
    all_gather x1, waiting for transfers between devices, on_device(): lax.all_gather(w_down, 'dp', axis=2, tiled=True)  28.4 us
    all_to_all x1, waiting for transfers between devices, on_device(): lax.all_to_all(routed_send, 'expert', split_axis=0, concat_axis=2, tiled=...  21 us
    all_to_all x1, waiting for transfers between devices, on_device(): lax.all_to_all(pair_grad[None], 'expert', split_axis=2, concat_axis=0, ti...  18 us
    mul x4, local copies, waits for them, and re-layouts, on_device(): gate_probs.astype(jnp.float32)[:, :, None]  8.63 us
  transfers between devices with their start and end apart: 10, of which 5 were waited for; matrix products, arithmetic and copies ran while one was open for 41% of the time, Pallas kernels for 0%

commit v1 on v0

--- a/solution.py
+++ b/solution.py
@@ -1,6 +1,10 @@
+import functools
+
 import jax
 import jax.numpy as jnp
 from jax import lax
+from jax.experimental import pallas as pl
+from jax.experimental.pallas import tpu as pltpu
 from jax.sharding import PartitionSpec as P
 
 
@@ -9,7 +13,7 @@
     return (pre_gate * sigma, sigma * (1.0 + pre_gate * (1.0 - sigma)))
 
 
-def on_device(tokens, cotangent, expert_ids, gate_probs, w_gate, w_up, w_down):
+def on_device_routed(tokens, cotangent, expert_ids, gate_probs, w_gate, w_up, w_down):
     axis_count = lax.axis_size("expert")
     local_experts = w_gate.shape[0]
     tok_rows = tokens.shape[0]
@@ -22,7 +26,10 @@
     onehot = (flat_ids[:, None] == jnp.arange(all_experts, dtype=jnp.int32)[None, :]).astype(
         jnp.int32
     )
-    earlier = jnp.cumsum(onehot, axis=0) - onehot
+    before = jnp.tril(jnp.ones((pair_count, pair_count), jnp.bfloat16), -1)
+    earlier = jnp.dot(
+        before, onehot.astype(jnp.bfloat16), preferred_element_type=jnp.float32
+    ).astype(jnp.int32)
     slot_rank = jnp.sum(earlier * onehot, axis=1)
     position = flat_ids * capacity + slot_rank
     pair_table = jnp.full((all_experts * capacity,), pair_count, jnp.int32)
@@ -102,7 +109,370 @@
     return (mixed, grad_tokens, grad_gates, grad_gate_w, grad_up_w, grad_down_w)
 
 
+MESH = pl.DeviceIdType.MESH
+CHIPS = 4
+
+
+def places():
+    q, e = lax.axis_index("dp"), lax.axis_index("expert")
+    z, c = e // 2, e % 2
+    x, y = q % 2, q // 2
+    xn, yn, dn = 2 * y + 1 - x, 2 * (1 - y) + x, 2 * (1 - y) + 1 - x
+    return q, e, z, c, xn, yn, dn
+
+
+def greet(q, e, z, c, dp_peers):
+    barrier = pltpu.get_barrier_semaphore()
+
+    def hello(dev):
+        pl.semaphore_signal(barrier, inc=1, device_id=dev, device_id_type=MESH)
+
+    pl.when(z > 0)(lambda: hello((q, e - 2)))
+    pl.when(z < CHIPS - 1)(lambda: hello((q, e + 2)))
+    hello((q, 2 * z + 1 - c))
+    for p in dp_peers:
+        hello((p, e))
+    line = jnp.where(z > 0, 1, 0) + jnp.where(z < CHIPS - 1, 1, 0)
+    pl.semaphore_wait(barrier, line + (1 + len(dp_peers)))
+
+
+def remote(src, dst, send, recv, dev):
+    return pltpu.make_async_remote_copy(
+        src_ref=src, dst_ref=dst, send_sem=send, recv_sem=recv, device_id=dev, device_id_type=MESH
+    )
+
+
+def shard_of(ref, q, start=0, rows=None):
+    rows = ref.shape[-2] if rows is None else rows
+    if len(ref.shape) == 3:
+        return ref.at[q, pl.ds(start, rows)]
+    width = ref.shape[1] // 4
+    return ref.at[pl.ds(start, rows), pl.ds(pl.multiple_of(q * width, 128), width)]
+
+
+def gather_kernel(*refs):
+    ins, ws = refs[0:3], refs[3:6]
+    alls, wall = refs[6:9], refs[9:12]
+    own_sem, w_own, line_s, line_r, sib_s, sib_r, ws_s, ws_r = refs[12:]
+    q, e, z, c, xn, yn, dn = places()
+    sib = (q, 2 * z + 1 - c)
+    greet(q, e, z, c, (xn, yn))
+
+    half = ws[0].shape[0] // 2
+    w_sends = []
+    for w in range(3):
+        for k, p in enumerate((xn, yn)):
+            cp = remote(ws[w], shard_of(wall[w], q), ws_s.at[w, k], ws_r.at[w, k], (p, e))
+            cp.start()
+            w_sends.append(cp)
+
+    def block(a, zs, core):
+        return alls[a].at[2 * zs + core]
+
+    def source(a, zs, d):
+        return ins[a] if d == 0 else block(a, zs, c)
+
+    def line_copy(a, dr, d):
+        zs, to = (z - d, e + 2) if dr == 0 else (z + d, e - 2)
+        return remote(
+            source(a, zs, d), block(a, zs, c), line_s.at[a, dr, d], line_r.at[a, dr, d], (q, to)
+        )
+
+    def sib_copy(a, dr, d):
+        zs = z - d if dr == 0 else z + d
+        return remote(source(a, zs, d), block(a, zs, c), sib_s.at[a, dr, d], sib_r.at[a, dr, d], sib)
+
+    def has_block(dr, d):
+        return z - d >= 0 if dr == 0 else z + d <= CHIPS - 1
+
+    def forwards(dr, d):
+        return (
+            jnp.logical_and(z - d >= 0, z < CHIPS - 1)
+            if dr == 0
+            else jnp.logical_and(z + d <= CHIPS - 1, z > 0)
+        )
+
+    locals_ = []
+    for d in range(CHIPS):
+        for a in range(3):
+            for dr in range(2):
+                if d > 0:
+
+                    @pl.when(has_block(dr, d))
+                    def _():
+                        zs = z - d if dr == 0 else z + d
+                        remote(
+                            block(a, zs, c),
+                            block(a, zs, c),
+                            line_s.at[a, dr, d - 1],
+                            line_r.at[a, dr, d - 1],
+                            sib,
+                        ).wait_recv()
+
+                if d < CHIPS - 1:
+                    pl.when(forwards(dr, d))(lambda: line_copy(a, dr, d).start())
+                if d > 0:
+                    pl.when(has_block(dr, d))(lambda: sib_copy(a, dr, d).start())
+                elif dr == 0:
+                    sib_copy(a, 0, 0).start()
+        if d == 0:
+            for a in range(3):
+                cp = pltpu.make_async_copy(ins[a], alls[a].at[e], own_sem.at[a])
+                cp.start()
+                locals_.append(cp)
+            for w in range(3):
+                cp = pltpu.make_async_copy(ws[w], shard_of(wall[w], q), w_own.at[w])
+                cp.start()
+                locals_.append(cp)
+        if d == 1:
+            for w in range(3):
+                for k, (p, other) in enumerate(((xn, yn), (yn, xn))):
+                    whole = shard_of(wall[w], p)
+                    remote(whole, whole, ws_s.at[w, k], ws_r.at[w, k], (p, e)).wait_recv()
+                    part = shard_of(wall[w], p, half * k, half)
+                    cp = remote(part, part, ws_s.at[w, 2 + k], ws_r.at[w, 2 + k], (other, e))
+                    cp.start()
+                    w_sends.append(cp)
+    for cp in locals_:
+        cp.wait()
+    for w in range(3):
+        for k in range(2):
+            part = shard_of(wall[w], dn, half * k, half)
+            remote(part, part, ws_s.at[w, 2 + k], ws_r.at[w, 2 + k], (xn, e)).wait_recv()
+    for cp in w_sends:
+        cp.wait_send()
+    for d in range(CHIPS):
+        for a in range(3):
+            for dr in range(2):
+                if d < CHIPS - 1:
+                    pl.when(forwards(dr, d))(lambda: line_copy(a, dr, d).wait_send())
+                if d == 0 and dr == 1:
+                    continue
+
+                @pl.when(has_block(dr, d))
+                def _():
+                    zs = z - d if dr == 0 else z + d
+                    sib_copy(a, dr, d).wait_send()
+                    got = block(a, zs, 1 - c)
+                    remote(got, got, sib_s.at[a, dr, d], sib_r.at[a, dr, d], sib).wait_recv()
+
+
+def gather_all(tokens, cotangent, weights_t, w_gate, w_up, w_down):
+    rows, width = tokens.shape
+    n = weights_t.shape[0]
+    depth, hid = w_gate.shape
+    any_ = pl.BlockSpec(memory_space=pl.ANY)
+    dma = pltpu.SemaphoreType.DMA
+    return pl.pallas_call(
+        gather_kernel,
+        out_shape=(
+            jax.ShapeDtypeStruct((n, rows, width), tokens.dtype),
+            jax.ShapeDtypeStruct((n, rows, width), tokens.dtype),
+            jax.ShapeDtypeStruct((n,) + weights_t.shape, weights_t.dtype),
+            jax.ShapeDtypeStruct((4, depth, hid), w_gate.dtype),
+            jax.ShapeDtypeStruct((4, depth, hid), w_gate.dtype),
+            jax.ShapeDtypeStruct((hid, 4 * depth), w_gate.dtype),
+        ),
+        in_specs=[any_] * 6,
+        out_specs=(any_,) * 6,
+        scratch_shapes=[
+            dma((3,)),
+            dma((3,)),
+            dma((3, 2, 3)),
+            dma((3, 2, 3)),
+            dma((3, 2, 4)),
+            dma((3, 2, 4)),
+            dma((3, 4)),
+            dma((3, 4)),
+        ],
+        compiler_params=pltpu.CompilerParams(collective_id=0, has_side_effects=True),
+    )(tokens, cotangent, weights_t, w_gate, w_up, w_down)
+
+
+def reduce_kernel(*refs):
+    parts, wp = refs[0:3], refs[3:6]
+    outs, wout = refs[6:9], refs[9:12]
+    srecv, lrecv, wrecv = refs[12:15], refs[15:18], refs[18:21]
+    sib_s, sib_r, line_s, line_r, w_s, w_r = refs[21:]
+    q, e, z, c, xn, yn, dn = places()
+    sib = (q, 2 * z + 1 - c)
+    peers = (xn, yn, dn)
+    greet(q, e, z, c, peers)
+
+    def sib_copy(a, i):
+        dest = CHIPS - 1 - i // 2 if i % 2 == 0 else i // 2
+        return remote(
+            parts[a].at[2 * dest + 1 - c], srecv[a].at[dest], sib_s.at[a, dest], sib_r.at[a, dest], sib
+        )
+
+    for i in range(CHIPS):
+        for a in range(3):
+            sib_copy(a, i).start()
+    w_copies = []
+    for w in range(3):
+        for k, p in enumerate(peers):
+            cp = remote(shard_of(wp[w], p), wrecv[w].at[k], w_s.at[w, k], w_r.at[w, k], (p, e))
+            cp.start()
+            w_copies.append(cp)
+
+    def wait_sib(a, dest):
+        remote(
+            srecv[a].at[dest], srecv[a].at[dest], sib_s.at[a, dest], sib_r.at[a, dest], sib
+        ).wait_recv()
+
+    def wait_line(a, dr, dest):
+        ref = lrecv[a].at[dr, dest]
+        remote(ref, ref, line_s.at[a, dr, dest], line_r.at[a, dr, dest], sib).wait_recv()
+
+    def line_copy(a, dr, dest):
+        return remote(
+            srecv[a].at[dest],
+            lrecv[a].at[dr, dest],
+            line_s.at[a, dr, dest],
+            line_r.at[a, dr, dest],
+            (q, e + 2 if dr == 0 else e - 2),
+        )
+
+    def add_into(out, terms):
+        rows = out.shape[0]
+        step = min(rows, 16)
+
+        @pl.loop(0, rows // step)
+        def _(i):
+            at = pl.ds(pl.multiple_of(i * step, step), step)
+            total = terms[0][at, :].astype(jnp.float32)
+            for t in terms[1:]:
+                total = total + t[at, :].astype(jnp.float32)
+            out[at, :] = total.astype(out.dtype)
+
+    for i in range(CHIPS - 1):
+        for a in range(3):
+            for dr in range(2):
+                dest = CHIPS - 1 - i if dr == 0 else i
+                inner = z > 0 if dr == 0 else z < CHIPS - 1
+
+                @pl.when(dest > z if dr == 0 else dest < z)
+                def _():
+                    wait_sib(a, dest)
+                    mine, held = parts[a].at[2 * dest + c], srecv[a].at[dest]
+
+                    @pl.when(inner)
+                    def _():
+                        wait_line(a, dr, dest)
+                        add_into(held, (mine, held, lrecv[a].at[dr, dest]))
+
+                    @pl.when(jnp.logical_not(inner))
+                    def _():
+                        add_into(held, (mine, held))
+
+                    line_copy(a, dr, dest).start()
+
+    for w in range(3):
+        for k in range(3):
+            w_copies[3 * w + k].wait_recv()
+        add_into(wout[w], (shard_of(wp[w], q),) + tuple(wrecv[w].at[k] for k in range(3)))
+
+    for a in range(3):
+        wait_sib(a, z)
+        mine, other = parts[a].at[2 * z + c], srecv[a].at[z]
+
+        @pl.when(z == 0)
+        def _():
+            wait_line(a, 1, z)
+            add_into(outs[a], (mine, other, lrecv[a].at[1, z]))
+
+        @pl.when(z == CHIPS - 1)
+        def _():
+            wait_line(a, 0, z)
+            add_into(outs[a], (mine, other, lrecv[a].at[0, z]))
+
+        @pl.when(jnp.logical_and(z > 0, z < CHIPS - 1))
+        def _():
+            wait_line(a, 0, z)
+            wait_line(a, 1, z)
+            add_into(outs[a], (mine, other, lrecv[a].at[0, z], lrecv[a].at[1, z]))
+
+    for cp in w_copies:
+        cp.wait_send()
+    for i in range(CHIPS):
+        for a in range(3):
+            sib_copy(a, i).wait_send()
+    for a in range(3):
+        for i in range(CHIPS - 1):
+            for dr in range(2):
+                dest = CHIPS - 1 - i if dr == 0 else i
+                pl.when(dest > z if dr == 0 else dest < z)(
+                    lambda: line_copy(a, dr, dest).wait_send()
+                )
+
+
+def reduce_all(parts, weight_parts):
+    n, rows, width = parts[0].shape
+    dma = pltpu.SemaphoreType.DMA
+    vmem = pl.BlockSpec(memory_space=pltpu.VMEM)
+    depth, hid = weight_parts[0].shape[1:]
+    shards = [(depth, hid), (depth, hid), (hid, depth)]
+    return pl.pallas_call(
+        reduce_kernel,
+        out_shape=tuple(jax.ShapeDtypeStruct(p.shape[1:], p.dtype) for p in parts)
+        + tuple(jax.ShapeDtypeStruct(s, jnp.float32) for s in shards),
+        in_specs=[vmem] * 6,
+        out_specs=(vmem,) * 6,
+        scratch_shapes=[pltpu.VMEM((CHIPS,) + p.shape[1:], p.dtype) for p in parts]
+        + [pltpu.VMEM((2, CHIPS) + p.shape[1:], p.dtype) for p in parts]
+        + [pltpu.VMEM((3,) + s, jnp.bfloat16) for s in shards]
+        + [dma((3, 4)), dma((3, 4)), dma((3, 2, 4)), dma((3, 2, 4)), dma((3, 3)), dma((3, 3))],
+        compiler_params=pltpu.CompilerParams(
+            collective_id=1, has_side_effects=True, vmem_limit_bytes=56 << 20
+        ),
+    )(*parts, *weight_parts)
+
+
+def on_device(tokens, cotangent, expert_ids, gate_probs, w_gate, w_up, w_down):
+    n = lax.axis_size("expert")
+    rows, width = tokens.shape
+    f32, bf16 = jnp.float32, jnp.bfloat16
+    me = lax.axis_index("expert")
+    named = expert_ids[None, :, :] == jnp.arange(n, dtype=jnp.int32)[:, None, None]
+    weights_t = jnp.sum(jnp.where(named, gate_probs.astype(f32)[None], 0.0), axis=2)
+    toks, cots, gates, full_gate, full_up, full_down = gather_all(
+        tokens, cotangent, weights_t, w_gate[0], w_up[0], w_down[0]
+    )
+    x = toks.reshape(n * rows, width)
+    cot = cots.reshape(n * rows, width)
+    wg = full_gate.reshape(width, -1)
+    wu = full_up.reshape(width, -1)
+    g = lax.dynamic_index_in_dim(gates, me, axis=1, keepdims=False).reshape(n * rows, 1)
+    dot = functools.partial(lax.dot_general, preferred_element_type=f32)
+    mm, nt, tn = (((1,), (0,)), ((), ())), (((1,), (1,)), ((), ())), (((0,), (0,)), ((), ()))
+    pre_gate = dot(x, wg, mm)
+    pre_up = dot(x, wu, mm)
+    back = dot(cot, full_down, nt)
+    activated, slope = silu_parts(pre_gate)
+    hidden = activated * pre_up
+    weighted = (g * hidden).astype(bf16)
+    gate_grad = jnp.sum(hidden * back, axis=1)
+    grad_hidden = g * back
+    grad_pre_gate = (grad_hidden * pre_up * slope).astype(bf16)
+    grad_pre_up = (grad_hidden * activated).astype(bf16)
+    part_mixed = dot(weighted, full_down, mm).astype(bf16).reshape(n, rows, width)
+    part_tokens = (dot(grad_pre_gate, wg, nt) + dot(grad_pre_up, wu, nt)).astype(bf16)
+    part_tokens = part_tokens.reshape(n, rows, width)
+    part_gates = jnp.where(
+        (jnp.arange(n) == me)[None, :, None], gate_grad.reshape(n, 1, rows), 0.0
+    )
+    part_gate_w = dot(x, grad_pre_gate, tn).astype(bf16).reshape(full_gate.shape)
+    part_up_w = dot(x, grad_pre_up, tn).astype(bf16).reshape(full_up.shape)
+    part_down_w = dot(weighted, cot, tn).astype(bf16)
+    mixed, grad_tokens, gates_all, gw, uw, dw = reduce_all(
+        (part_mixed, part_tokens, part_gates), (part_gate_w, part_up_w, part_down_w)
+    )
+    grad_gates = jnp.sum(jnp.where(named, gates_all[:, :, None], 0.0), axis=0)
+    return (mixed, grad_tokens, grad_gates, gw[None], uw[None], dw[None])
+
+
 def solution(mesh):
+    small = mesh.shape["expert"] == 2 * CHIPS and mesh.shape["dp"] == 4
     in_specs = (
         P(("dp", "expert"), None),
         P(("dp", "expert"), None),
@@ -121,5 +491,9 @@
         P("expert", None, "dp"),
     )
     return jax.shard_map(
-        on_device, mesh=mesh, in_specs=in_specs, out_specs=out_specs, check_vma=False
-    )
+        on_device if small else on_device_routed,
+        mesh=mesh,
+        in_specs=in_specs,
+        out_specs=out_specs,
+        check_vma=False,
+    )

time: 375 us -> 235 us (0.63)
  the two profiles are of different devices: /device:TPU:0 before, /device:TPU:20 now
where the time goes in v1:
time: 235 us; the launch traced here: 234 us
  Pallas kernels  188 us (80%)
  matrix products  33.5 us (14%)
  local copies, waits for them, and re-layouts  8.03 us (3%)
  other arithmetic  4.01 us (2%)
    pallas_call x1, Pallas kernels, reduce_all(): pl.pallas_call(reduce_kernel, out_shape=tuple((jax.ShapeDtypeStruct(p.sha...  104 us
    pallas_call x1, Pallas kernels, gather_all(): pl.pallas_call(gather_kernel, out_shape=(jax.ShapeDtypeStruct((n, rows, w...  83.3 us
    unnamed x23, local copies, waits for them, and re-layouts  7.25 us
    dot_general x1, matrix products, on_device(): pre_up = dot(x, wu, mm)  5.37 us

profile of v1, /device:TPU:20, one launch (start us, length us, event | category | flops | bytes accessed | tf_op | source)
XLA Modules:
  0.0 233.9 jit_solution(14530707064538484921)
XLA Ops:
  0.6 0.7 convert_element_type.27
  1.3 1.3 select_reduce_fusion.1.refs_2_
  2.6 83.3 %shard_map.118 = (bf16[8,128,2048]{2,1,0:T(8,128)(2,1)}, bf16[8,128,2048]{2,1,0:T(8,128)(2,1)}, f32[8,8,128]{2,1,0:T(8,128)}, bf16[4,512,512]{2,1,0:T(8,128)(2,1...) custom-call(bf16[128,2048]{1,0:T(8,128)(2,1)} %refs_0_.1, bf16[128,2048]{1,0:T(8,128)(2,1)} %refs_1_.1, ...), custom_call_target="tpu_custom_call" | custom-call | tf_op jit(solution)/shard_map/pallas_call | solution.py:266
  86.0 0.8 constant_dynamic-slice_fusion
  86.7 0.0 copy-start.4
  86.7 0.0 copy-start.7
  86.7 5.4 %fusion.2 = f32[1024,512]{0,1:T(8,128)S(1)} fusion(bf16[1024,2048]{1,0:T(8,128)(2,1)} %bitcast.46, bf16[2048,512]{1,0:T(8,128)(2,1)} %bitcast.52), kind=kOutput, calls=%fused_computation.18 | convolution fusion | flops 2147483648 | bytes 8388608 | tf_op jit(solution)/shard_map/dot_general | solution.py:449
  92.1 0.0 copy-done.4
  92.1 0.0 copy-done.7
  92.1 0.0 copy-start.5
  92.1 0.0 copy-start.8
  92.2 2.4 %fusion.1 = f32[1024,512]{0,1:T(8,128)S(1)} fusion(bf16[1024,2048]{1,0:T(8,128)(2,1)S(1)} %bitcast.47, bf16[2048,512]{1,0:T(8,128)(2,1)S(1)} %bitcast.54), kind=kOutput, calls=%fused_computation.17 | convolution fusion | flops 2147483648 | bytes 8388608 | tf_op jit(solution)/shard_map/dot_general | solution.py:448
  94.5 0.0 copy-done.5
  94.5 0.5 copy-done.8
  95.0 3.3 %multiply_reduce_fusion = (f32[1024]{0:T(1024)S(1)}, bf16[1024,512]{0,1:T(8,128)(2,1)S(1)}, bf16[1024,512]{0,1:T(8,128)(2,1)S(1)}, bf16[1024,512]{0,1:T(8,128)(2,1)S(1)}) fusion(f32[1024,512]{0,1:T(8,128)S(1)} %fusion.2, f32[1024,512]{0,1:T(8,128)S(1)} %fusion.1, f32[1024]{0:T(1024)S(1)} %bitcast.45, bf16[1024,2048]{1,0:T(8,128)(2,1)S(1)} %bitcast.50, ...), kind=kOutput, calls=%fused_computation.5 | convolution fusion | flops 2157444096 | bytes 13639680 | tf_op jit(solution)/shard_map/dot_general | solution.py:450
  98.3 3.7 %convolution_convert_fusion.1.refs_5_ = bf16[512,2048]{1,0:T(8,128)(2,1)} fusion(bf16[1024,512]{0,1:T(8,128)(2,1)S(1)} %get-tuple-element.32, bf16[1024,2048]{1,0:T(8,128)(2,1)S(1)} %bitcast.51), kind=kOutput, calls=%fused_computation.2 | convolution fusion | flops 2148532224 | bytes 7340032 | tf_op jit(solution)/shard_map/dot_general | solution.py:466
  102.0 0.7 broadcast_select_fusion.refs_2_
  102.6 4.0 %convolution_convert_fusion.3 = bf16[2048,512]{1,0:T(8,128)(2,1)} fusion(bf16[1024,2048]{1,0:T(8,128)(2,1)S(1)} %bitcast.48, bf16[1024,512]{0,1:T(8,128)(2,1)S(1)} %get-tuple-element.31), kind=kOutput, calls=%fused_computation.4 | convolution fusion | flops 2148532224 | bytes 7340032 | tf_op jit(solution)/shard_map/dot_general | solution.py:464
  106.6 3.7 %convolution_convert_fusion.2 = bf16[2048,512]{1,0:T(8,128)(2,1)} fusion(bf16[1024,2048]{1,0:T(8,128)(2,1)S(1)} %bitcast.49, bf16[1024,512]{0,1:T(8,128)(2,1)S(1)} %get-tuple-element.33), kind=kOutput, calls=%fused_computation.3 | convolution fusion | flops 2148532224 | bytes 7340032 | tf_op jit(solution)/shard_map/dot_general | solution.py:465
  110.3 4.3 %convolution_convert_fusion = bf16[1024,2048]{1,0:T(8,128)(2,1)} fusion(bf16[1024,512]{0,1:T(8,128)(2,1)S(1)} %get-tuple-element.32, bf16[512,2048]{1,0:T(8,128)(2,1)S(1)} %copy-done.8), kind=kOutput, calls=%fused_computation.1 | convolution fusion | flops 2149580800 | bytes 7340032 | tf_op jit(solution)/shard_map/dot_general | solution.py:458
  114.7 0.0 copy-start.6
  114.7 2.4 %fusion.3 = f32[1024,2048]{1,0:T(8,128)S(1)} fusion(bf16[1024,512]{0,1:T(8,128)(2,1)S(1)} %get-tuple-element.31, bf16[2048,512]{1,0:T(8,128)(2,1)S(1)} %bitcast.55), kind=kOutput, calls=%fused_computation.19 | convolution fusion | flops 2147483648 | bytes 11534336 | tf_op jit(solution)/shard_map/dot_general | solution.py:459
  117.1 0.0 copy-done.6
  117.1 4.4 %add_convert_fusion = bf16[1024,2048]{1,0:T(8,128)(2,1)} fusion(f32[1024,2048]{1,0:T(8,128)S(1)} %fusion.3, bf16[1024,512]{0,1:T(8,128)(2,1)S(1)} %get-tuple-element.33, bf16[2048,512]{1,0:T(8,128)(2,1)S(1)} %bitcast.53), kind=kOutput, calls=%fused_computation | convolution fusion | flops 2151677952 | bytes 15728640 | tf_op jit(solution)/shard_map/dot_general | solution.py:459
  121.5 0.0 copy-start.3
  121.5 104.3 %shard_map.119 = (bf16[128,2048]{1,0:T(8,128)(2,1)}, bf16[128,2048]{1,0:T(8,128)(2,1)}, f32[8,128]{1,0:T(8,128)}, f32[512,512]{1,0:T(8,128)}, f32[512,512]{1,0:T(8,128)}, /*index=5*/f32[512,512]{1,0:T(8,128)}) custom-call(bf16[8,128,2048]{2,1,0:T(8,128)(2,1)} %bitcast.34, bf16[8,128,2048]{2,1,0:T(8,128)(2,1)} %bitcast.35, ...), custom_call_target="tpu_custom_call" | custom-call | tf_op jit(solution)/shard_map/pallas_call | solution.py:415
  225.8 0.0 copy-start.2
  225.8 0.0 copy-done.3
  225.8 1.4 select_reduce_fusion
  227.2 0.0 copy-start.1
  227.2 2.0 copy.20
  229.1 1.9 copy.21
  231.0 0.0 copy-done.2
  231.0 0.0 copy-start
  231.0 1.0 copy.22
  232.0 0.0 copy-done.1
  232.0 1.0 copy.23
  233.0 0.0 copy-done
  233.0 1.0 copy.24
  (1 shorter events, 0.0 us)
Async XLA Ops:
  86.7 5.4 %copy-start.4 = (bf16[8,128,2048]{2,1,0:T(8,128)(2,1)S(1)}, bf16[8,128,2048]{2,1,0:T(8,128)(2,1)}, u32[]{:S(2)}) copy-start(bf16[8,128,2048]{2,1,0:T(8,128)(2,1)} %get-tuple-element.19) | copy-start | bytes 12582916
  86.7 5.4 %copy-start.7 = (bf16[4,512,512]{2,1,0:T(8,128)(2,1)S(1)}, bf16[4,512,512]{2,1,0:T(8,128)(2,1)}, u32[]{:S(2)}) copy-start(bf16[4,512,512]{2,1,0:T(8,128)(2,1)} %get-tuple-element.20) | copy-start | bytes 6291460
  92.1 2.4 %copy-start.5 = (bf16[8,128,2048]{2,1,0:T(8,128)(2,1)S(1)}, bf16[8,128,2048]{2,1,0:T(8,128)(2,1)}, u32[]{:S(2)}) copy-start(bf16[8,128,2048]{2,1,0:T(8,128)(2,1)} %get-tuple-element.23) | copy-start | bytes 12582916
  92.1 2.9 %copy-start.8 = (bf16[512,2048]{1,0:T(8,128)(2,1)S(1)}, bf16[512,2048]{1,0:T(8,128)(2,1)}, u32[]{:S(2)}) copy-start(bf16[512,2048]{1,0:T(8,128)(2,1)} %get-tuple-element.22) | copy-start | bytes 6291460
  114.7 2.4 %copy-start.6 = (bf16[4,512,512]{2,1,0:T(8,128)(2,1)S(1)}, bf16[4,512,512]{2,1,0:T(8,128)(2,1)}, u32[]{:S(2)}) copy-start(bf16[4,512,512]{2,1,0:T(8,128)(2,1)} %get-tuple-element.21) | copy-start | bytes 6291460
  121.5 104.4 %copy-start.3 = (s32[128,4]{0,1:T(4,128)S(1)}, s32[128,4]{0,1:T(4,128)}, u32[]{:S(2)}) copy-start(s32[128,4]{0,1:T(4,128)} %param.9) | copy-start | bytes 6148
  225.8 5.2 %copy-start.2 = (f32[512,512]{1,0:T(8,128)S(1)}, f32[512,512]{1,0:T(8,128)}, u32[]{:S(2)}) copy-start(f32[512,512]{1,0:T(8,128)} %get-tuple-element.27) | copy-start | bytes 3145732
  227.2 4.8 %copy-start.1 = (f32[512,512]{1,0:T(8,128)S(1)}, f32[512,512]{1,0:T(8,128)}, u32[]{:S(2)}) copy-start(f32[512,512]{1,0:T(8,128)} %get-tuple-element.28) | copy-start | bytes 3145732
  231.0 1.9 copy-start

commit v2 on v1

--- a/solution.py
+++ b/solution.py
@@ -296,8 +296,7 @@
     sib_s, sib_r, line_s, line_r, w_s, w_r = refs[21:]
     q, e, z, c, xn, yn, dn = places()
     sib = (q, 2 * z + 1 - c)
-    peers = (xn, yn, dn)
-    greet(q, e, z, c, peers)
+    greet(q, e, z, c, (xn, yn))
 
     def sib_copy(a, i):
         dest = CHIPS - 1 - i // 2 if i % 2 == 0 else i // 2
@@ -305,15 +304,24 @@
             parts[a].at[2 * dest + 1 - c], srecv[a].at[dest], sib_s.at[a, dest], sib_r.at[a, dest], sib
         )
 
-    for i in range(CHIPS):
-        for a in range(3):
-            sib_copy(a, i).start()
+    def start_sib(a, pair):
+        sib_copy(a, 2 * pair).start()
+        sib_copy(a, 2 * pair + 1).start()
+
+    half = wout[0].shape[0] // 2
     w_copies = []
-    for w in range(3):
-        for k, p in enumerate(peers):
-            cp = remote(shard_of(wp[w], p), wrecv[w].at[k], w_s.at[w, k], w_r.at[w, k], (p, e))
-            cp.start()
-            w_copies.append(cp)
+
+    def w_send(w, slot, src, p):
+        cp = remote(src, wrecv[w].at[slot], w_s.at[w, slot], w_r.at[w, slot], (p, e))
+        cp.start()
+        w_copies.append(cp)
+
+    def w_got(w, slot):
+        ref = wrecv[w].at[slot]
+        remote(ref, ref, w_s.at[w, slot], w_r.at[w, slot], (xn, e)).wait_recv()
+        return ref
+
+    start_sib(0, 0)
 
     def wait_sib(a, dest):
         remote(
@@ -348,6 +356,20 @@
     for i in range(CHIPS - 1):
         for a in range(3):
             for dr in range(2):
+                if i == 0 and dr == 0:
+                    if a == 0:
+                        start_sib(1, 0)
+                        start_sib(2, 0)
+                        for w in range(3):
+                            w_send(w, 1, shard_of(wp[w], dn, 0, half), xn)
+                            w_send(w, 3, shard_of(wp[w], dn, half, half), yn)
+                            w_send(w, 0, shard_of(wp[w], xn, 0, half), xn)
+                            w_send(w, 2, shard_of(wp[w], yn, half, half), yn)
+                    elif a == 1:
+                        start_sib(0, 1)
+                    else:
+                        start_sib(1, 1)
+                        start_sib(2, 1)
                 dest = CHIPS - 1 - i if dr == 0 else i
                 inner = z > 0 if dr == 0 else z < CHIPS - 1
 
@@ -367,10 +389,19 @@
 
                     line_copy(a, dr, dest).start()
 
+        if i == 0:
+            for w in range(3):
+                held = wrecv[w].at[6]
+                add_into(held, (shard_of(wp[w], yn, 0, half), w_got(w, 1)))
+                w_send(w, 4, held, yn)
+                held = wrecv[w].at[7]
+                add_into(held, (shard_of(wp[w], xn, half, half), w_got(w, 3)))
+                w_send(w, 5, held, xn)
+
     for w in range(3):
-        for k in range(3):
-            w_copies[3 * w + k].wait_recv()
-        add_into(wout[w], (shard_of(wp[w], q),) + tuple(wrecv[w].at[k] for k in range(3)))
+        for k in range(2):
+            terms = (shard_of(wp[w], q, half * k, half), w_got(w, 2 * k), w_got(w, 4 + k))
+            add_into(wout[w].at[pl.ds(half * k, half)], terms)
 
     for a in range(3):
         wait_sib(a, z)
@@ -420,8 +451,8 @@
         out_specs=(vmem,) * 6,
         scratch_shapes=[pltpu.VMEM((CHIPS,) + p.shape[1:], p.dtype) for p in parts]
         + [pltpu.VMEM((2, CHIPS) + p.shape[1:], p.dtype) for p in parts]
-        + [pltpu.VMEM((3,) + s, jnp.bfloat16) for s in shards]
-        + [dma((3, 4)), dma((3, 4)), dma((3, 2, 4)), dma((3, 2, 4)), dma((3, 3)), dma((3, 3))],
+        + [pltpu.VMEM((8, s[0] // 2, s[1]), jnp.bfloat16) for s in shards]
+        + [dma((3, 4)), dma((3, 4)), dma((3, 2, 4)), dma((3, 2, 4)), dma((3, 6)), dma((3, 6))],
         compiler_params=pltpu.CompilerParams(
             collective_id=1, has_side_effects=True, vmem_limit_bytes=56 << 20
         ),

time: 235 us -> 236 us (level)
  no operation moved by 1% of the time
where the time goes in v2:
time: 236 us; the launch traced here: 235 us
  Pallas kernels  189 us (80%)
  matrix products  33.5 us (14%)
  local copies, waits for them, and re-layouts  8.03 us (3%)
  other arithmetic  4.01 us (2%)
    pallas_call x1, Pallas kernels, reduce_all(): pl.pallas_call(reduce_kernel, out_shape=tuple((jax.ShapeDtypeStruct(p.sha...  106 us
    pallas_call x1, Pallas kernels, gather_all(): pl.pallas_call(gather_kernel, out_shape=(jax.ShapeDtypeStruct((n, rows, w...  83.3 us
    unnamed x23, local copies, waits for them, and re-layouts  7.25 us
    dot_general x1, matrix products, on_device(): pre_up = dot(x, wu, mm)  5.37 us

profile of v2, /device:TPU:20, one launch (start us, length us, event | category | flops | bytes accessed | tf_op | source)
XLA Modules:
  0.0 235.3 jit_solution(8758489421648507327)
XLA Ops:
  0.6 0.7 convert_element_type.27
  1.3 1.3 select_reduce_fusion.1.refs_2_
  2.6 83.3 %shard_map.118 = (bf16[8,128,2048]{2,1,0:T(8,128)(2,1)}, bf16[8,128,2048]{2,1,0:T(8,128)(2,1)}, f32[8,8,128]{2,1,0:T(8,128)}, bf16[4,512,512]{2,1,0:T(8,128)(2,1...) custom-call(bf16[128,2048]{1,0:T(8,128)(2,1)} %refs_0_.1, bf16[128,2048]{1,0:T(8,128)(2,1)} %refs_1_.1, ...), custom_call_target="tpu_custom_call" | custom-call | tf_op jit(solution)/shard_map/pallas_call | solution.py:266
  86.0 0.8 constant_dynamic-slice_fusion
  86.7 0.0 copy-start.4
  86.7 0.0 copy-start.7
  86.7 5.4 %fusion.2 = f32[1024,512]{0,1:T(8,128)S(1)} fusion(bf16[1024,2048]{1,0:T(8,128)(2,1)} %bitcast.46, bf16[2048,512]{1,0:T(8,128)(2,1)} %bitcast.52), kind=kOutput, calls=%fused_computation.18 | convolution fusion | flops 2147483648 | bytes 8388608 | tf_op jit(solution)/shard_map/dot_general | solution.py:480
  92.1 0.0 copy-done.4
  92.1 0.0 copy-done.7
  92.1 0.0 copy-start.5
  92.1 0.0 copy-start.8
  92.2 2.4 %fusion.1 = f32[1024,512]{0,1:T(8,128)S(1)} fusion(bf16[1024,2048]{1,0:T(8,128)(2,1)S(1)} %bitcast.47, bf16[2048,512]{1,0:T(8,128)(2,1)S(1)} %bitcast.54), kind=kOutput, calls=%fused_computation.17 | convolution fusion | flops 2147483648 | bytes 8388608 | tf_op jit(solution)/shard_map/dot_general | solution.py:479
  94.5 0.0 copy-done.5
  94.5 0.5 copy-done.8
  95.0 3.3 %multiply_reduce_fusion = (f32[1024]{0:T(1024)S(1)}, bf16[1024,512]{0,1:T(8,128)(2,1)S(1)}, bf16[1024,512]{0,1:T(8,128)(2,1)S(1)}, bf16[1024,512]{0,1:T(8,128)(2,1)S(1)}) fusion(f32[1024,512]{0,1:T(8,128)S(1)} %fusion.2, f32[1024,512]{0,1:T(8,128)S(1)} %fusion.1, f32[1024]{0:T(1024)S(1)} %bitcast.45, bf16[1024,2048]{1,0:T(8,128)(2,1)S(1)} %bitcast.50, ...), kind=kOutput, calls=%fused_computation.5 | convolution fusion | flops 2157444096 | bytes 13639680 | tf_op jit(solution)/shard_map/dot_general | solution.py:481
  98.3 3.7 %convolution_convert_fusion.1.refs_5_ = bf16[512,2048]{1,0:T(8,128)(2,1)} fusion(bf16[1024,512]{0,1:T(8,128)(2,1)S(1)} %get-tuple-element.32, bf16[1024,2048]{1,0:T(8,128)(2,1)S(1)} %bitcast.51), kind=kOutput, calls=%fused_computation.2 | convolution fusion | flops 2148532224 | bytes 7340032 | tf_op jit(solution)/shard_map/dot_general | solution.py:497
  102.0 0.7 broadcast_select_fusion.refs_2_
  102.6 4.0 %convolution_convert_fusion.3 = bf16[2048,512]{1,0:T(8,128)(2,1)} fusion(bf16[1024,2048]{1,0:T(8,128)(2,1)S(1)} %bitcast.48, bf16[1024,512]{0,1:T(8,128)(2,1)S(1)} %get-tuple-element.31), kind=kOutput, calls=%fused_computation.4 | convolution fusion | flops 2148532224 | bytes 7340032 | tf_op jit(solution)/shard_map/dot_general | solution.py:495
  106.6 3.7 %convolution_convert_fusion.2 = bf16[2048,512]{1,0:T(8,128)(2,1)} fusion(bf16[1024,2048]{1,0:T(8,128)(2,1)S(1)} %bitcast.49, bf16[1024,512]{0,1:T(8,128)(2,1)S(1)} %get-tuple-element.33), kind=kOutput, calls=%fused_computation.3 | convolution fusion | flops 2148532224 | bytes 7340032 | tf_op jit(solution)/shard_map/dot_general | solution.py:496
  110.3 4.3 %convolution_convert_fusion = bf16[1024,2048]{1,0:T(8,128)(2,1)} fusion(bf16[1024,512]{0,1:T(8,128)(2,1)S(1)} %get-tuple-element.32, bf16[512,2048]{1,0:T(8,128)(2,1)S(1)} %copy-done.8), kind=kOutput, calls=%fused_computation.1 | convolution fusion | flops 2149580800 | bytes 7340032 | tf_op jit(solution)/shard_map/dot_general | solution.py:489
  114.7 0.0 copy-start.6
  114.7 2.4 %fusion.3 = f32[1024,2048]{1,0:T(8,128)S(1)} fusion(bf16[1024,512]{0,1:T(8,128)(2,1)S(1)} %get-tuple-element.31, bf16[2048,512]{1,0:T(8,128)(2,1)S(1)} %bitcast.55), kind=kOutput, calls=%fused_computation.19 | convolution fusion | flops 2147483648 | bytes 11534336 | tf_op jit(solution)/shard_map/dot_general | solution.py:490
  117.1 0.0 copy-done.6
  117.1 4.4 %add_convert_fusion = bf16[1024,2048]{1,0:T(8,128)(2,1)} fusion(f32[1024,2048]{1,0:T(8,128)S(1)} %fusion.3, bf16[1024,512]{0,1:T(8,128)(2,1)S(1)} %get-tuple-element.33, bf16[2048,512]{1,0:T(8,128)(2,1)S(1)} %bitcast.53), kind=kOutput, calls=%fused_computation | convolution fusion | flops 2151677952 | bytes 15728640 | tf_op jit(solution)/shard_map/dot_general | solution.py:490
  121.5 0.0 copy-start.3
  121.5 105.7 %shard_map.119 = (bf16[128,2048]{1,0:T(8,128)(2,1)}, bf16[128,2048]{1,0:T(8,128)(2,1)}, f32[8,128]{1,0:T(8,128)}, f32[512,512]{1,0:T(8,128)}, f32[512,512]{1,0:T(8,128)}, /*index=5*/f32[512,512]{1,0:T(8,128)}) custom-call(bf16[8,128,2048]{2,1,0:T(8,128)(2,1)} %bitcast.34, bf16[8,128,2048]{2,1,0:T(8,128)(2,1)} %bitcast.35, ...), custom_call_target="tpu_custom_call" | custom-call | tf_op jit(solution)/shard_map/pallas_call | solution.py:446
  227.2 0.0 copy-start.2
  227.2 0.0 copy-done.3
  227.2 1.4 select_reduce_fusion
  228.5 0.0 copy-start.1
  228.5 2.0 copy.20
  230.5 1.9 copy.21
  232.4 0.0 copy-done.2
  232.4 0.0 copy-start
  232.4 1.0 copy.22
  233.4 0.0 copy-done.1
  233.4 1.0 copy.23
  234.3 0.0 copy-done
  234.3 1.0 copy.24
  (1 shorter events, 0.0 us)
Async XLA Ops:
  86.7 5.4 %copy-start.4 = (bf16[8,128,2048]{2,1,0:T(8,128)(2,1)S(1)}, bf16[8,128,2048]{2,1,0:T(8,128)(2,1)}, u32[]{:S(2)}) copy-start(bf16[8,128,2048]{2,1,0:T(8,128)(2,1)} %get-tuple-element.19) | copy-start | bytes 12582916
  86.7 5.4 %copy-start.7 = (bf16[4,512,512]{2,1,0:T(8,128)(2,1)S(1)}, bf16[4,512,512]{2,1,0:T(8,128)(2,1)}, u32[]{:S(2)}) copy-start(bf16[4,512,512]{2,1,0:T(8,128)(2,1)} %get-tuple-element.20) | copy-start | bytes 6291460
  92.1 2.4 %copy-start.5 = (bf16[8,128,2048]{2,1,0:T(8,128)(2,1)S(1)}, bf16[8,128,2048]{2,1,0:T(8,128)(2,1)}, u32[]{:S(2)}) copy-start(bf16[8,128,2048]{2,1,0:T(8,128)(2,1)} %get-tuple-element.23) | copy-start | bytes 12582916
  92.1 2.9 %copy-start.8 = (bf16[512,2048]{1,0:T(8,128)(2,1)S(1)}, bf16[512,2048]{1,0:T(8,128)(2,1)}, u32[]{:S(2)}) copy-start(bf16[512,2048]{1,0:T(8,128)(2,1)} %get-tuple-element.22) | copy-start | bytes 6291460
  114.7 2.4 %copy-start.6 = (bf16[4,512,512]{2,1,0:T(8,128)(2,1)S(1)}, bf16[4,512,512]{2,1,0:T(8,128)(2,1)}, u32[]{:S(2)}) copy-start(bf16[4,512,512]{2,1,0:T(8,128)(2,1)} %get-tuple-element.21) | copy-start | bytes 6291460
  121.5 105.7 %copy-start.3 = (s32[128,4]{0,1:T(4,128)S(1)}, s32[128,4]{0,1:T(4,128)}, u32[]{:S(2)}) copy-start(s32[128,4]{0,1:T(4,128)} %param.9) | copy-start | bytes 6148
  227.2 5.2 %copy-start.2 = (f32[512,512]{1,0:T(8,128)S(1)}, f32[512,512]{1,0:T(8,128)}, u32[]{:S(2)}) copy-start(f32[512,512]{1,0:T(8,128)} %get-tuple-element.27) | copy-start | bytes 3145732
  228.5 4.8 %copy-start.1 = (f32[512,512]{1,0:T(8,128)S(1)}, f32[512,512]{1,0:T(8,128)}, u32[]{:S(2)}) copy-start(f32[512,512]{1,0:T(8,128)} %get-tuple-element.28) | copy-start | bytes 3145732
  232.4 1.9 copy-start

commit v3 on v2

--- a/solution.py
+++ b/solution.py
@@ -387,6 +387,8 @@
                     def _():
                         add_into(held, (mine, held))
 
+                    if i > 0:
+                        line_copy(a, dr, dest + 1 if dr == 0 else dest - 1).wait_send()
                     line_copy(a, dr, dest).start()
 
         if i == 0:
@@ -432,7 +434,7 @@
         for i in range(CHIPS - 1):
             for dr in range(2):
                 dest = CHIPS - 1 - i if dr == 0 else i
-                pl.when(dest > z if dr == 0 else dest < z)(
+                pl.when(dest == z + 1 if dr == 0 else dest == z - 1)(
                     lambda: line_copy(a, dr, dest).wait_send()
                 )
 

time: 236 us -> 236 us (level)
  no operation moved by 1% of the time
where the time goes in v3:
time: 236 us; the launch traced here: 235 us
  Pallas kernels  189 us (80%)
  matrix products  33.5 us (14%)
  local copies, waits for them, and re-layouts  8.03 us (3%)
  other arithmetic  4.01 us (2%)
    pallas_call x1, Pallas kernels, reduce_all(): pl.pallas_call(reduce_kernel, out_shape=tuple((jax.ShapeDtypeStruct(p.sha...  106 us
    pallas_call x1, Pallas kernels, gather_all(): pl.pallas_call(gather_kernel, out_shape=(jax.ShapeDtypeStruct((n, rows, w...  83.3 us
    unnamed x23, local copies, waits for them, and re-layouts  7.25 us
    dot_general x1, matrix products, on_device(): pre_up = dot(x, wu, mm)  5.37 us

profile of v3, /device:TPU:20, one launch (start us, length us, event | category | flops | bytes accessed | tf_op | source)
XLA Modules:
  0.0 235.3 jit_solution(16702634949552432093)
XLA Ops:
  0.6 0.7 convert_element_type.27
  1.3 1.3 select_reduce_fusion.1.refs_2_
  2.6 83.3 %shard_map.118 = (bf16[8,128,2048]{2,1,0:T(8,128)(2,1)}, bf16[8,128,2048]{2,1,0:T(8,128)(2,1)}, f32[8,8,128]{2,1,0:T(8,128)}, bf16[4,512,512]{2,1,0:T(8,128)(2,1...) custom-call(bf16[128,2048]{1,0:T(8,128)(2,1)} %refs_0_.1, bf16[128,2048]{1,0:T(8,128)(2,1)} %refs_1_.1, ...), custom_call_target="tpu_custom_call" | custom-call | tf_op jit(solution)/shard_map/pallas_call | solution.py:266
  86.0 0.8 constant_dynamic-slice_fusion
  86.7 0.0 copy-start.4
  86.7 0.0 copy-start.7
  86.7 5.4 %fusion.2 = f32[1024,512]{0,1:T(8,128)S(1)} fusion(bf16[1024,2048]{1,0:T(8,128)(2,1)} %bitcast.46, bf16[2048,512]{1,0:T(8,128)(2,1)} %bitcast.52), kind=kOutput, calls=%fused_computation.18 | convolution fusion | flops 2147483648 | bytes 8388608 | tf_op jit(solution)/shard_map/dot_general | solution.py:482
  92.1 0.0 copy-done.4
  92.1 0.0 copy-done.7
  92.1 0.0 copy-start.5
  92.1 0.0 copy-start.8
  92.2 2.4 %fusion.1 = f32[1024,512]{0,1:T(8,128)S(1)} fusion(bf16[1024,2048]{1,0:T(8,128)(2,1)S(1)} %bitcast.47, bf16[2048,512]{1,0:T(8,128)(2,1)S(1)} %bitcast.54), kind=kOutput, calls=%fused_computation.17 | convolution fusion | flops 2147483648 | bytes 8388608 | tf_op jit(solution)/shard_map/dot_general | solution.py:481
  94.5 0.0 copy-done.5
  94.5 0.5 copy-done.8
  95.0 3.3 %multiply_reduce_fusion = (f32[1024]{0:T(1024)S(1)}, bf16[1024,512]{0,1:T(8,128)(2,1)S(1)}, bf16[1024,512]{0,1:T(8,128)(2,1)S(1)}, bf16[1024,512]{0,1:T(8,128)(2,1)S(1)}) fusion(f32[1024,512]{0,1:T(8,128)S(1)} %fusion.2, f32[1024,512]{0,1:T(8,128)S(1)} %fusion.1, f32[1024]{0:T(1024)S(1)} %bitcast.45, bf16[1024,2048]{1,0:T(8,128)(2,1)S(1)} %bitcast.50, ...), kind=kOutput, calls=%fused_computation.5 | convolution fusion | flops 2157444096 | bytes 13639680 | tf_op jit(solution)/shard_map/dot_general | solution.py:483
  98.3 3.7 %convolution_convert_fusion.1.refs_5_ = bf16[512,2048]{1,0:T(8,128)(2,1)} fusion(bf16[1024,512]{0,1:T(8,128)(2,1)S(1)} %get-tuple-element.32, bf16[1024,2048]{1,0:T(8,128)(2,1)S(1)} %bitcast.51), kind=kOutput, calls=%fused_computation.2 | convolution fusion | flops 2148532224 | bytes 7340032 | tf_op jit(solution)/shard_map/dot_general | solution.py:499
  102.0 0.7 broadcast_select_fusion.refs_2_
  102.6 4.0 %convolution_convert_fusion.3 = bf16[2048,512]{1,0:T(8,128)(2,1)} fusion(bf16[1024,2048]{1,0:T(8,128)(2,1)S(1)} %bitcast.48, bf16[1024,512]{0,1:T(8,128)(2,1)S(1)} %get-tuple-element.31), kind=kOutput, calls=%fused_computation.4 | convolution fusion | flops 2148532224 | bytes 7340032 | tf_op jit(solution)/shard_map/dot_general | solution.py:497
  106.6 3.7 %convolution_convert_fusion.2 = bf16[2048,512]{1,0:T(8,128)(2,1)} fusion(bf16[1024,2048]{1,0:T(8,128)(2,1)S(1)} %bitcast.49, bf16[1024,512]{0,1:T(8,128)(2,1)S(1)} %get-tuple-element.33), kind=kOutput, calls=%fused_computation.3 | convolution fusion | flops 2148532224 | bytes 7340032 | tf_op jit(solution)/shard_map/dot_general | solution.py:498
  110.3 4.3 %convolution_convert_fusion = bf16[1024,2048]{1,0:T(8,128)(2,1)} fusion(bf16[1024,512]{0,1:T(8,128)(2,1)S(1)} %get-tuple-element.32, bf16[512,2048]{1,0:T(8,128)(2,1)S(1)} %copy-done.8), kind=kOutput, calls=%fused_computation.1 | convolution fusion | flops 2149580800 | bytes 7340032 | tf_op jit(solution)/shard_map/dot_general | solution.py:491
  114.7 0.0 copy-start.6
  114.7 2.4 %fusion.3 = f32[1024,2048]{1,0:T(8,128)S(1)} fusion(bf16[1024,512]{0,1:T(8,128)(2,1)S(1)} %get-tuple-element.31, bf16[2048,512]{1,0:T(8,128)(2,1)S(1)} %bitcast.55), kind=kOutput, calls=%fused_computation.19 | convolution fusion | flops 2147483648 | bytes 11534336 | tf_op jit(solution)/shard_map/dot_general | solution.py:492
  117.1 0.0 copy-done.6
  117.1 4.4 %add_convert_fusion = bf16[1024,2048]{1,0:T(8,128)(2,1)} fusion(f32[1024,2048]{1,0:T(8,128)S(1)} %fusion.3, bf16[1024,512]{0,1:T(8,128)(2,1)S(1)} %get-tuple-element.33, bf16[2048,512]{1,0:T(8,128)(2,1)S(1)} %bitcast.53), kind=kOutput, calls=%fused_computation | convolution fusion | flops 2151677952 | bytes 15728640 | tf_op jit(solution)/shard_map/dot_general | solution.py:492
  121.5 0.0 copy-start.3
  121.5 105.7 %shard_map.119 = (bf16[128,2048]{1,0:T(8,128)(2,1)}, bf16[128,2048]{1,0:T(8,128)(2,1)}, f32[8,128]{1,0:T(8,128)}, f32[512,512]{1,0:T(8,128)}, f32[512,512]{1,0:T(8,128)}, /*index=5*/f32[512,512]{1,0:T(8,128)}) custom-call(bf16[8,128,2048]{2,1,0:T(8,128)(2,1)} %bitcast.34, bf16[8,128,2048]{2,1,0:T(8,128)(2,1)} %bitcast.35, ...), custom_call_target="tpu_custom_call" | custom-call | tf_op jit(solution)/shard_map/pallas_call | solution.py:448
  227.2 0.0 copy-start.2
  227.2 0.0 copy-done.3
  227.2 1.4 select_reduce_fusion
  228.5 0.0 copy-start.1
  228.5 2.0 copy.20
  230.5 1.9 copy.21
  232.4 0.0 copy-done.2
  232.4 0.0 copy-start
  232.4 1.0 copy.22
  233.4 0.0 copy-done.1
  233.4 1.0 copy.23
  234.3 0.0 copy-done
  234.3 1.0 copy.24
  (1 shorter events, 0.0 us)
Async XLA Ops:
  86.7 5.4 %copy-start.4 = (bf16[8,128,2048]{2,1,0:T(8,128)(2,1)S(1)}, bf16[8,128,2048]{2,1,0:T(8,128)(2,1)}, u32[]{:S(2)}) copy-start(bf16[8,128,2048]{2,1,0:T(8,128)(2,1)} %get-tuple-element.19) | copy-start | bytes 12582916
  86.7 5.4 %copy-start.7 = (bf16[4,512,512]{2,1,0:T(8,128)(2,1)S(1)}, bf16[4,512,512]{2,1,0:T(8,128)(2,1)}, u32[]{:S(2)}) copy-start(bf16[4,512,512]{2,1,0:T(8,128)(2,1)} %get-tuple-element.20) | copy-start | bytes 6291460
  92.1 2.4 %copy-start.5 = (bf16[8,128,2048]{2,1,0:T(8,128)(2,1)S(1)}, bf16[8,128,2048]{2,1,0:T(8,128)(2,1)}, u32[]{:S(2)}) copy-start(bf16[8,128,2048]{2,1,0:T(8,128)(2,1)} %get-tuple-element.23) | copy-start | bytes 12582916
  92.1 2.9 %copy-start.8 = (bf16[512,2048]{1,0:T(8,128)(2,1)S(1)}, bf16[512,2048]{1,0:T(8,128)(2,1)}, u32[]{:S(2)}) copy-start(bf16[512,2048]{1,0:T(8,128)(2,1)} %get-tuple-element.22) | copy-start | bytes 6291460
  114.7 2.4 %copy-start.6 = (bf16[4,512,512]{2,1,0:T(8,128)(2,1)S(1)}, bf16[4,512,512]{2,1,0:T(8,128)(2,1)}, u32[]{:S(2)}) copy-start(bf16[4,512,512]{2,1,0:T(8,128)(2,1)} %get-tuple-element.21) | copy-start | bytes 6291460
  121.5 105.7 %copy-start.3 = (s32[128,4]{0,1:T(4,128)S(1)}, s32[128,4]{0,1:T(4,128)}, u32[]{:S(2)}) copy-start(s32[128,4]{0,1:T(4,128)} %param.9) | copy-start | bytes 6148
  227.2 5.2 %copy-start.2 = (f32[512,512]{1,0:T(8,128)S(1)}, f32[512,512]{1,0:T(8,128)}, u32[]{:S(2)}) copy-start(f32[512,512]{1,0:T(8,128)} %get-tuple-element.27) | copy-start | bytes 3145732
  228.5 4.8 %copy-start.1 = (f32[512,512]{1,0:T(8,128)S(1)}, f32[512,512]{1,0:T(8,128)}, u32[]{:S(2)}) copy-start(f32[512,512]{1,0:T(8,128)} %get-tuple-element.28) | copy-start | bytes 3145732
  232.4 1.9 copy-start
